TPU v7x, 256 devices: a whole 4x4x8 slice. The times are simulated.
256 devices in a mesh: ctx: 8 (over z), expert: 32 (over y, x, core).
Axes of the slice: x: 4, y: 4, z: 8, core: 2. Of those that a mesh axis runs over, the one named last changes fastest.
Arguments:
- tokens: bfloat16 [32, 1024, 1024], P('expert', 'ctx'), may hold values from -6 to 6
- chain_ids: int32 [32, 1024], P('expert', 'ctx'), may hold values from 0 to 7, never falling along the last dimension, each value on 1 to 256 neighbouring positions
- route_ids: int32 [32, 1024, 6], P('expert', 'ctx'), may hold values from 0 to 31, all different within a row; in each aligned block of 128 rows (0 to 127, 128 to 255, ..., all dimensions but the last counted through in order) at most 32 rows name the same one
- route_weights: float32 [32, 1024, 6], P('expert', 'ctx'), may hold values from 0.1 to 0.5
- attn_gain: float32 [1024], replicated, may hold values from 0.6 to 12
- ffn_gain: float32 [1024], replicated, may hold values from 0.1 to 1.9
- chain_bias: float32 [8], replicated, may hold values from 0.5 to 2.5
- w_qkv: bfloat16 [3, 1024, 1024], P(None, 'expert', 'ctx'), may hold values from -0.1875 to 0.1875
- w_out: bfloat16 [1024, 1024], P('ctx', 'expert'), may hold values from -0.75 to 0.75
- w_gateup: bfloat16 [32, 1024, 2816], P('expert'), may hold values from -0.1875 to 0.1875
- w_down: bfloat16 [32, 1408, 1024], P('expert'), may hold values from -0.15625 to 0.15625
Outputs:
- layer_out: bfloat16 [32, 1024, 1024], P('expert', 'ctx')
Inputs may be any that keep to these rules, and one draw needn't show every extreme that they name: `route_ids`: each residue names 6 different experts. Among the 128 residues of one device (aligned blocks of the residues in order, crop after crop), no expert is named by more than 32 of them, and in every draw some expert is named by exactly 32. `chain_ids`: chain numbers never fall along a crop; a chain spans 1 to 256 residues, and some chain exactly that many.
All inputs are finite; a program needn't handle non-finite values.
Results may differ from a plain program's by a relative error of at most 0.02.
The roundings to bfloat16 on the way count: a program that leaves them out, or rounds other values in their place, can miss the bound.
Values may be sent and summed in bfloat16 or wider, within the bound.
No kernel may reach another device: no remote copies, remote signals or barrier semaphores. Data moves between devices by JAX's collectives and lax.ppermute only.
A program may use at most 64 MiB of HBM per device.

v0:
```python
import math
import jax
import jax.numpy as jnp
from jax import lax
from jax.sharding import PartitionSpec as P


def rms_scale(values, gain):
    wide = values.astype(jnp.float32)
    return wide * lax.rsqrt(jnp.mean(wide * wide, axis=-1, keepdims=True) + 1e-05) * gain


def attend(query, key, value, chains, bias):
    length = query.shape[0]
    group = bias.shape[0]
    head_dim = query.shape[1] // group
    block = min(512, length)
    scale = 1.0 / math.sqrt(head_dim)
    keys = key.reshape(length, group, head_dim)
    values = value.reshape(length, group, head_dim)
    query_blocks = query.reshape(length // block, block, group, head_dim)
    chain_blocks = chains.reshape(length // block, block)

    def one_block(items):
        q_block, c_block = items
        scores = (
            jnp.einsum("qhd,khd->hqk", q_block, keys, preferred_element_type=jnp.float32) * scale
        )
        same = (c_block[:, None] == chains[None, :]).astype(jnp.float32)
        scores = scores + bias[:, None, None] * same[None]
        top = jnp.max(scores, axis=-1, keepdims=True)
        raised = jnp.exp(scores - top)
        probs = (raised / jnp.sum(raised, axis=-1, keepdims=True)).astype(jnp.bfloat16)
        return jnp.einsum("hqk,khd->qhd", probs, values, preferred_element_type=jnp.float32).astype(
            jnp.bfloat16
        )

    return lax.map(one_block, (query_blocks, chain_blocks)).reshape(length, group * head_dim)


def per_device(
    tokens,
    chain_ids,
    route_ids,
    route_weights,
    attn_gain,
    ffn_gain,
    chain_bias,
    w_qkv,
    w_out,
    w_gateup,
    w_down,
):
    tok = tokens.shape[1]
    width = tokens.shape[2]
    inputs = tokens[0]
    normed = rms_scale(inputs, attn_gain).astype(jnp.bfloat16)
    chains = lax.all_gather(chain_ids[0], "ctx", axis=0, tiled=True)
    groups = lax.axis_size("ctx")
    per_group = chain_bias.shape[0] // groups
    bias = lax.dynamic_slice_in_dim(chain_bias, lax.axis_index("ctx") * per_group, per_group)
    qkv_columns, out_full_rows = (
        lax.all_gather(w_qkv, "ctx", axis=2, tiled=True),
        lax.all_gather(w_out, "ctx", axis=0, tiled=True),
    )
    projected = jnp.einsum(
        "tr,ird->itd",
        normed,
        lax.all_gather(qkv_columns, "expert", axis=1, tiled=True),
        preferred_element_type=jnp.float32,
    ).astype(jnp.bfloat16)
    regrouped = lax.all_to_all(projected, "ctx", split_axis=2, concat_axis=1, tiled=True)
    attended = attend(regrouped[0], regrouped[1], regrouped[2], chains, bias)
    local_rows = lax.all_to_all(attended, "ctx", split_axis=0, concat_axis=1, tiled=True)
    mixed = inputs.astype(jnp.float32) + jnp.dot(
        local_rows,
        lax.all_gather(out_full_rows, "expert", axis=1, tiled=True),
        preferred_element_type=jnp.float32,
    )
    ffn_in = rms_scale(mixed, ffn_gain).astype(jnp.bfloat16)
    held = w_gateup.shape[0]
    experts = lax.axis_size("expert") * held
    topk = route_ids.shape[2]
    cap = min(tok, tok * topk * 4 // (experts * 3))
    hidden = w_down.shape[1]
    flat_ids = route_ids[0].reshape(-1)
    onehot = (flat_ids[:, None] == jnp.arange(experts, dtype=jnp.int32)[None, :]).astype(jnp.int32)
    rank = jnp.sum((jnp.cumsum(onehot, axis=0) - onehot) * onehot, axis=1)
    slots = flat_ids * cap + rank
    select = jnp.sum(
        (
            slots.reshape(tok, topk)[:, :, None]
            == jnp.arange(experts * cap, dtype=jnp.int32)[None, None, :]
        ).astype(jnp.bfloat16),
        axis=1,
    )
    outgoing = lax.dot_general(
        select, ffn_in, (((0,), (0,)), ((), ())), preferred_element_type=jnp.float32
    )
    outgoing = outgoing.astype(jnp.bfloat16).reshape(experts, cap, width)
    block = lax.all_to_all(outgoing, "expert", split_axis=0, concat_axis=0, tiled=True)
    count = block.shape[1]
    grouped = block.reshape(-1, held, count, width)
    both = jnp.einsum("sxcd,xdf->sxcf", grouped, w_gateup, preferred_element_type=jnp.float32)
    active = (jax.nn.silu(both[..., :hidden]) * both[..., hidden:]).astype(jnp.bfloat16)
    result = jnp.einsum(
        "sxcf,xfd->sxcd", active, w_down, preferred_element_type=jnp.float32
    ).astype(jnp.bfloat16)
    returned = lax.all_to_all(
        result.reshape(-1, count, width), "expert", split_axis=0, concat_axis=0, tiled=True
    )
    picked = jnp.take(returned.reshape(-1, width), slots, axis=0).reshape(tok, topk, width)
    weights = route_weights[0]
    moe_sum = mixed
    for route in range(topk):
        moe_sum = moe_sum + weights[:, route : route + 1] * picked[:, route].astype(jnp.float32)
    return moe_sum.astype(jnp.bfloat16)[None]


def solution(mesh):
    placed = (
        P("expert", "ctx", None),
        P("expert", "ctx"),
        P("expert", "ctx", None),
        P("expert", "ctx", None),
        P(),
        P(),
        P(),
        P(None, "expert", "ctx"),
        P("ctx", "expert"),
        P("expert", None, None),
        P("expert", None, None),
    )
    return jax.shard_map(
        per_device, mesh=mesh, in_specs=placed, out_specs=P("expert", "ctx", None), check_vma=False
    )
```

profile of v0, /device:TPU:1, one launch (start us, length us, event | category | flops | bytes accessed | tf_op | source)
XLA Modules:
  0.0 299.5 jit_solution(6906347522959631811)
XLA Ops:
  6.5 23.7 %all_gather.15 = bf16[3,32,1024]{2,1,0:T(8,128)(2,1)} all-gather(bf16[3,32,128]{2,1,0:T(8,128)(2,1)} %param.20), channel_id=1, replica_groups=mesh['ctx'=8,'expert'=32] {'ctx'}, dimensions={2}, use_global_device_ids=true | all-gather | bytes 221184 | tf_op jit(solution)/shard_map/all_gather | solution.py:63
  30.3 1.1 fusion.22
  31.4 57.7 %all-gather.4.cloned.1.call-done = bf16[3,1024,1024]{2,1,0:T(8,128)(2,1)} async-done(((bf16[3,32,1024]{2,1,0:T(8,128)(2,1)}), bf16[3,1024,1024]{2,1,0:T(8,128)(2,1)}) %all-gather.4.cloned.1.call-update) | async-done | bytes 6291472 | tf_op jit(solution)/shard_map/all_gather | solution.py:69
  89.0 4.8 %fusion.21 = bf16[3,128,1024]{2,1,0:T(8,128)(2,1)} fusion(bf16[3,1024,1024]{2,1,0:T(8,128)(2,1)} %all-gather.4.cloned.1.call-done, bf16[1,128,1024]{2,1,0:T(8,128)(2,1)} %param.13, f32[1024]{0:T(1024)} %param.17, f32[128]{0:T(128)S(1)} %add_rsqrt_fusion.1), kind=kOutput, calls=%fused_computation.28 | convolution fusion | flops 806223872 | bytes 7344640 | tf_op jit(solution)/shard_map/tr,ird->itd/dot_general | solution.py:66
  93.9 2.4 copy.69
  96.3 6.7 %all-to-all-start = ((bf16[3,128,1024]{1,0,2:T(4,128)(2,1)}), bf16[3,128,1024]{1,0,2:T(4,128)(2,1)}, u32[]{:S(2)}, u32[]{:S(2)}) async-start(bf16[3,128,1024]{1,0,2:T(4,128)(2,1)} %copy.69), calls=%async_computation | async-start | bytes 2097152 | tf_op jit(solution)/shard_map/all_to_all | solution.py:72
  103.1 39.4 %all_gather.18 = bf16[1024,32]{0,1:T(8,128)(2,1)} all-gather(bf16[128,32]{0,1:T(8,128)(2,1)S(1)} %copy-done.6), channel_id=1, replica_groups=mesh['ctx'=8,'expert'=32] {'ctx'}, dimensions={0}, use_global_device_ids=true | all-gather | bytes 73728 | tf_op jit(solution)/shard_map/all_gather | solution.py:64
  142.6 0.1 copy.77
  142.7 0.1 eq.54
  142.8 0.1 reshape_squeeze.15
  143.0 11.5 %all-gather = s32[1,1024]{1,0:T(1,128)S(1)} all-gather(s32[1,128]{1,0:T(1,128)S(1)} %copy-done.9), channel_id=2, replica_groups=mesh['ctx'=8,'expert'=32] {'ctx'}, dimensions={1}, use_global_device_ids=true | all-gather | bytes 4608 | tf_op jit(solution)/shard_map/all_gather | solution.py:58
  154.5 0.5 broadcast.132
  155.0 0.7 reduce.12
  155.7 1.7 reduce-window.6
  157.4 0.3 slice_reduce_fusion
  157.7 0.6 dynamic_slice.11
  158.3 1.3 copy.70
  159.7 0.8 fusion.47
  160.5 1.8 copy.71
  162.3 0.8 copy.72
  163.1 0.8 copy.73
  164.0 8.2 %while.10 = (s32[]{:T(128)}, bf16[2,512,1,128]{3,1,2,0:T(8,128)(2,1)}, bf16[2,512,1,128]{3,1,2,0:T(8,128)(2,1)}, bf16[1024,1,128]{2,0,1:T(8,128)(2,1)}, s32[2,51...) while((s32[]{:T(128)}, ...), condition=%wide.region_4.5_spmd, body=%wide.region_1.4_spmd.sunk | while | flops 273742848 | bytes 10245305 | solution.py:38
  164.0 2.3 fusion.58
  166.3 0.5 fusion.59
  166.8 0.6 fusion.60
  167.4 0.7 copy-done.3
  168.1 2.3 fusion.58
  170.4 0.5 fusion.59
  170.9 0.6 fusion.60
  171.5 0.7 copy-done.3
  172.2 4.2 %all-to-all-start.1 = ((bf16[8,128,128]{2,1,0:T(8,128)(2,1)}), bf16[8,128,128]{2,1,0:T(8,128)(2,1)S(1)}, u32[]{:S(2)}, u32[]{:S(2)}) async-start(bf16[8,128,128]{2,1,0:T(8,128)(2,1)} %bitcast.176), calls=%async_computation.1 | async-start | bytes 524288 | tf_op jit(solution)/shard_map/all_to_all | solution.py:74
  176.5 0.1 reduce_sum.54
  176.8 1.1 fusion.20
  177.9 7.9 %all-to-all-done.1 = bf16[8,128,128]{2,1,0:T(8,128)(2,1)S(1)} async-done(((bf16[8,128,128]{2,1,0:T(8,128)(2,1)}), bf16[8,128,128]{2,1,0:T(8,128)(2,1)S(1)}, u32[]{:S(2)}, u32[]{:S(2)}) %all-to-all-start.1) | async-done | bytes 262176 | tf_op jit(solution)/shard_map/all_to_all | solution.py:74
  185.8 0.9 copy.75
  186.6 6.5 %all-gather.6.cloned.1.call-done = bf16[1024,1024]{0,1:T(8,128)(2,1)} async-done(((bf16[1024,32]{0,1:T(8,128)(2,1)}), bf16[1024,1024]{0,1:T(8,128)(2,1)}) %all-gather.6.cloned.1.call-update) | async-done | bytes 2097168 | tf_op jit(solution)/shard_map/all_gather | solution.py:77
  193.2 2.6 multiply_reduce_fusion
  195.8 0.8 convolution_convert_fusion.1
  196.6 37.6 %all_to_all.44 = bf16[32,32,1024]{2,1,0:T(8,128)(2,1)S(1)} all-to-all(bf16[32,32,1024]{2,1,0:T(8,128)(2,1)S(1)} %bitcast.172), channel_id=1, replica_groups=mesh['ctx'=8,'expert'=32] {'expert'}, dimensions={0} | all-to-all | bytes 4194304 | tf_op jit(solution)/shard_map/all_to_all | solution.py:101
  234.2 6.1 %convolution_bitcast_fusion = f32[32,1,32,2816]{3,2,0,1:T(8,128)S(1)} fusion(bf16[32,32,1024]{2,1,0:T(8,128)(2,1)S(1)} %all_to_all.44, bf16[1,1024,2816]{2,1,0:T(8,128)(2,1)S(1)} %copy-done.10), kind=kOutput, calls=%fused_computation.14 | convolution fusion | flops 5905580032 | bytes 19398656 | tf_op jit(solution)/shard_map/sxcd,xdf->sxcf/dot_general | solution.py:104
  240.4 4.8 %fusion.15 = bf16[32,32,1024]{2,1,0:T(8,128)(2,1)} fusion(bf16[1,1408,1024]{2,1,0:T(8,128)(2,1)S(1)} %copy-done, f32[32,1,32,2816]{3,2,0,1:T(8,128)S(1)} %convolution_bitcast_fusion), kind=kOutput, calls=%fused_computation.23 | convolution fusion | flops 2962489344 | bytes 16515072 | tf_op jit(solution)/shard_map/sxcf,xfd->sxcd/dot_general | solution.py:106
  245.2 4.9 %all-to-all-start.3 = ((bf16[32,32,1024]{2,1,0:T(8,128)(2,1)}), bf16[32,32,1024]{2,1,0:T(8,128)(2,1)}, u32[]{:S(2)}, u32[]{:S(2)}) async-start(bf16[32,32,1024]{2,1,0:T(8,128)(2,1)} %fusion.15), calls=%async_computation.3 | async-start | bytes 4194304 | tf_op jit(solution)/shard_map/all_to_all | solution.py:109
  250.2 0.1 mul.167
  250.4 27.6 %all-to-all-done.3 = bf16[32,32,1024]{2,1,0:T(8,128)(2,1)} async-done(((bf16[32,32,1024]{2,1,0:T(8,128)(2,1)}), bf16[32,32,1024]{2,1,0:T(8,128)(2,1)}, u32[]{:S(2)}, u32[]{:S(2)}) %all-to-all-start.3) | async-done | bytes 2097184 | tf_op jit(solution)/shard_map/all_to_all | solution.py:109
  278.0 6.4 %gather_fusion = bf16[768,1024]{1,0:T(8,128)(2,1)} fusion(bf16[1024,1024]{1,0:T(8,128)(2,1)} %bitcast.38, s32[1024]{0:T(1024)S(1)} %pad_clamp_fusion), kind=kCustom, calls=%fused_computation | custom fusion | bytes 3148800 | tf_op jit(solution)/shard_map/jit(_take)/gather | solution.py:112
  284.4 3.7 %gather.7 = bf16[128,6,1024]{2,1,0:T(8,128)(2,1)} reshape(bf16[768,1024]{1,0:T(8,128)(2,1)} %gather_fusion) | data formatting | bytes 3145728 | tf_op jit(solution)/shard_map/jit(_take)/gather | solution.py:112
  288.1 3.4 %copy_select_fusion = bf16[128,6,1024]{2,0,1:T(8,128)(2,1)S(1)} fusion(bf16[128,6,1024]{2,1,0:T(8,128)(2,1)} %gather.7, pred[128,6]{0,1:T(8,128)(4,1)S(1)} %get-tuple-element.112), kind=kLoop, calls=%fused_computation.26 | loop fusion | flops 786432 | bytes 3146496 | tf_op jit(solution)/shard_map/jit(_take)/select_n | solution.py:112
  291.6 1.1 fusion.39
  (50 shorter events, 0.5 us)
Async XLA Ops:
  6.5 233.8 %copy-start = (bf16[1,1408,1024]{2,1,0:T(8,128)(2,1)S(1)}, bf16[1,1408,1024]{2,1,0:T(8,128)(2,1)}, u32[]{:S(2)}) copy-start(bf16[1,1408,1024]{2,1,0:T(8,128)(2,1)} %param.23) | copy-start | bytes 8650756
  6.5 82.5 %all-gather.4.cloned.1.call-start = ((), (), s32[]{:S(2)}) async-start(), calls=%async_computation.4 | async-start | bytes 6488064 | tf_op jit(solution)/shard_map/all_gather | solution.py:69
  93.9 9.2 %copy-start.6 = (bf16[128,32]{0,1:T(8,128)(2,1)S(1)}, bf16[128,32]{0,1:T(8,128)(2,1)}, u32[]{:S(2)}) copy-start(bf16[128,32]{0,1:T(8,128)(2,1)} %param.21) | copy-start | bytes 24580
  93.9 48.7 %copy-start.5 = (s32[1,128,6]{1,0,2:T(1,128)S(1)}, s32[1,128,6]{1,0,2:T(1,128)}, u32[]{:S(2)}) copy-start(s32[1,128,6]{1,0,2:T(1,128)} %param.15) | copy-start | bytes 9220
  93.9 49.1 %copy-start.9 = (s32[1,128]{1,0:T(1,128)S(1)}, s32[1,128]{1,0:T(1,128)}, u32[]{:S(2)}) copy-start(s32[1,128]{1,0:T(1,128)} %param.14) | copy-start | bytes 1540
  93.9 63.8 %copy-start.11 = (f32[8]{0:T(128)S(1)}, f32[8]{0:T(128)}, u32[]{:S(2)}) copy-start(f32[8]{0:T(128)} %param.19) | copy-start | bytes 100
  96.3 62.0 %all-to-all-start = ((bf16[3,128,1024]{1,0,2:T(4,128)(2,1)}), bf16[3,128,1024]{1,0,2:T(4,128)(2,1)}, u32[]{:S(2)}, u32[]{:S(2)}) async-start(bf16[3,128,1024]{1,0,2:T(4,128)(2,1)} %copy.69), calls=%async_computation | async-start | bytes 2097152 | tf_op jit(solution)/shard_map/all_to_all | solution.py:72
  103.0 90.1 %all-gather.6.cloned.1.call-start = ((), (), s32[]{:S(2)}) async-start(), calls=%async_computation.5 | async-start | bytes 2162688 | tf_op jit(solution)/shard_map/all_gather | solution.py:77
  164.0 2.8 copy-start.2
  164.0 2.8 copy-start.4
  167.4 0.7 copy-start.3
  168.1 2.8 copy-start.2
  168.1 2.8 copy-start.4
  171.5 0.7 copy-start.3
  172.2 13.6 %all-to-all-start.1 = ((bf16[8,128,128]{2,1,0:T(8,128)(2,1)}), bf16[8,128,128]{2,1,0:T(8,128)(2,1)S(1)}, u32[]{:S(2)}, u32[]{:S(2)}) async-start(bf16[8,128,128]{2,1,0:T(8,128)(2,1)} %bitcast.176), calls=%async_computation.1 | async-start | bytes 524288 | tf_op jit(solution)/shard_map/all_to_all | solution.py:74
  176.4 19.4 %copy-start.7 = (f32[1024]{0:T(1024)S(1)}, f32[1024]{0:T(1024)}, u32[]{:S(2)}) copy-start(f32[1024]{0:T(1024)} %param.18) | copy-start | bytes 12292
  193.2 2.6 copy-start.1
  195.8 38.4 %copy-start.10 = (bf16[1,1024,2816]{2,1,0:T(8,128)(2,1)S(1)}, bf16[1,1024,2816]{2,1,0:T(8,128)(2,1)}, u32[]{:S(2)}) copy-start(bf16[1,1024,2816]{2,1,0:T(8,128)(2,1)} %param.22) | copy-start | bytes 17301508
  245.2 5.2 %copy-start.8 = (f32[1,128,6]{1,0,2:T(1,128)S(1)}, f32[1,128,6]{1,0,2:T(1,128)}, u32[]{:S(2)}) copy-start(f32[1,128,6]{1,0,2:T(1,128)} %param.16) | copy-start | bytes 9220
  245.2 32.9 %all-to-all-start.3 = ((bf16[32,32,1024]{2,1,0:T(8,128)(2,1)}), bf16[32,32,1024]{2,1,0:T(8,128)(2,1)}, u32[]{:S(2)}, u32[]{:S(2)}) async-start(bf16[32,32,1024]{2,1,0:T(8,128)(2,1)} %fusion.15), calls=%async_computation.3 | async-start | bytes 4194304 | tf_op jit(solution)/shard_map/all_to_all | solution.py:109
Sparse Core Ops, SparseCore 0:
  30.4 58.5 all-gather.3
  142.7 50.4 all-gather.5
where the time goes:
time: 300 us
  blocking collectives  112 us (37%)
  waiting for transfers between devices  99.7 us (33%)
  matrix products  24.9 us (8%)
  local copies, waits for them, and re-layouts  22.7 us (8%)
  starting transfers between devices  15.9 us (5%)
  between operations  13.6 us (5%)
  other arithmetic  10.4 us (3%)
    all_gather x1, waiting for transfers between devices, per_device(): lax.all_gather(qkv_columns, 'expert', axis=1, tiled=True)  57.7 us
    all_gather x1, blocking collectives, per_device(): lax.all_gather(w_out, 'ctx', axis=0, tiled=True)  39.4 us
    all_to_all x1, blocking collectives, per_device(): lax.all_to_all(outgoing, 'expert', split_axis=0, concat_axis=0, tiled=True)  37.6 us
    all_to_all x1, waiting for transfers between devices, per_device(): lax.all_to_all(result.reshape(-1, count, width), 'expert', split_axis=0,...  27.6 us
    all_gather x1, blocking collectives, per_device(): lax.all_gather(w_qkv, 'ctx', axis=2, tiled=True)  23.7 us
    all_gather x1, blocking collectives, per_device(): chains = lax.all_gather(chain_ids[0], 'ctx', axis=0, tiled=True)  11.5 us
    gather x2, local copies, waits for them, and re-layouts, per_device(): jnp.take(returned.reshape(-1, width), slots, axis=0)  10.1 us
    all_to_all x1, waiting for transfers between devices, per_device(): lax.all_to_all(attended, 'ctx', split_axis=0, concat_axis=1, tiled=True)  7.86 us
  transfers between devices with their start and end apart: 5, of which 4 were waited for; matrix products, arithmetic and copies ran while one was open for 7% of the time, Pallas kernels for 0%

commit v1 on v0

--- a/solution.py
+++ b/solution.py
@@ -69,7 +69,10 @@
         lax.all_gather(qkv_columns, "expert", axis=1, tiled=True),
         preferred_element_type=jnp.float32,
     ).astype(jnp.bfloat16)
-    regrouped = lax.all_to_all(projected, "ctx", split_axis=2, concat_axis=1, tiled=True)
+    regrouped = jnp.concatenate(
+        lax.all_to_all(jnp.stack(jnp.split(projected, lax.axis_size("ctx"), axis=2)), "ctx", 0, 0),
+        axis=1,
+    )
     attended = attend(regrouped[0], regrouped[1], regrouped[2], chains, bias)
     local_rows = lax.all_to_all(attended, "ctx", split_axis=0, concat_axis=1, tiled=True)
     mixed = inputs.astype(jnp.float32) + jnp.dot(

time: 300 us -> 296 us (0.987)
  blocking collectives: 112 us -> 102 us
  waiting for transfers between devices: 99.7 us -> 104 us
    all_gather x1, blocking collectives: 39.4 us -> 33.8 us  [per_device(): lax.all_gather(w_out, 'ctx', axis=0, tiled=True)]
    all_gather x1, waiting for transfers between devices: 6.53 us -> 11.2 us  [per_device(): lax.all_gather(out_full_rows, 'expert', axis=1, tiled=True)]
    unnamed x20 -> x25, local copies, waits for them, and re-layouts: 0.15 us -> 4.75 us
    all_to_all x1, blocking collectives: 37.6 us -> 33.3 us  [per_device(): lax.all_to_all(outgoing, 'expert', split_axis=0, concat_axis=0, tiled=True)]
  transfers between devices with their start and end apart: 5 -> 5, of which waited for: 4 -> 4; matrix products, arithmetic and copies ran while one was open for 7% -> 6% of each run, Pallas kernels for 0% -> 0%
where the time goes in v1:
time: 296 us; the launch traced here: 294 us
  waiting for transfers between devices  104 us (35%)
  blocking collectives  102 us (34%)
  matrix products  27.4 us (9%)
  local copies, waits for them, and re-layouts  20.4 us (7%)
  starting transfers between devices  15.8 us (5%)
  between operations  13.7 us (5%)
  other arithmetic  10.4 us (4%)
    all_gather x1, waiting for transfers between devices, per_device(): lax.all_gather(qkv_columns, 'expert', axis=1, tiled=True)  57.7 us
    all_gather x1, blocking collectives, per_device(): lax.all_gather(w_out, 'ctx', axis=0, tiled=True)  33.8 us
    all_to_all x1, blocking collectives, per_device(): lax.all_to_all(outgoing, 'expert', split_axis=0, concat_axis=0, tiled=True)  33.3 us
    all_to_all x1, waiting for transfers between devices, per_device(): lax.all_to_all(result.reshape(-1, count, width), 'expert', split_axis=0,...  27.6 us
    all_gather x1, blocking collectives, per_device(): lax.all_gather(w_qkv, 'ctx', axis=2, tiled=True)  23.7 us
    all_gather x1, blocking collectives, per_device(): chains = lax.all_gather(chain_ids[0], 'ctx', axis=0, tiled=True)  11.5 us
    all_gather x1, waiting for transfers between devices, per_device(): lax.all_gather(out_full_rows, 'expert', axis=1, tiled=True)  11.2 us
    gather x2, local copies, waits for them, and re-layouts, per_device(): jnp.take(returned.reshape(-1, width), slots, axis=0)  10.1 us
  transfers between devices with their start and end apart: 5, of which 4 were waited for; matrix products, arithmetic and copies ran while one was open for 6% of the time, Pallas kernels for 0%

profile of v1, /device:TPU:1, one launch (start us, length us, event | category | flops | bytes accessed | tf_op | source)
XLA Modules:
  0.0 294.3 jit_solution(15124264526540278522)
XLA Ops:
  6.5 23.7 %all_gather.15 = bf16[3,32,1024]{2,1,0:T(8,128)(2,1)} all-gather(bf16[3,32,128]{2,1,0:T(8,128)(2,1)} %param.20), channel_id=1, replica_groups=mesh['ctx'=8,'expert'=32] {'ctx'}, dimensions={2}, use_global_device_ids=true | all-gather | bytes 221184 | tf_op jit(solution)/shard_map/all_gather | solution.py:63
  30.3 1.1 fusion.22
  31.4 57.7 %all-gather.4.cloned.1.call-done = bf16[3,1024,1024]{2,1,0:T(8,128)(2,1)} async-done(((bf16[3,32,1024]{2,1,0:T(8,128)(2,1)}), bf16[3,1024,1024]{2,1,0:T(8,128)(2,1)}) %all-gather.4.cloned.1.call-update) | async-done | bytes 6291472 | tf_op jit(solution)/shard_map/all_gather | solution.py:69
  89.0 3.9 %fusion.21 = bf16[3,128,1024]{2,1,0:T(8,128)(2,1)S(1)} fusion(bf16[3,1024,1024]{2,1,0:T(8,128)(2,1)} %all-gather.4.cloned.1.call-done, bf16[1,128,1024]{2,1,0:T(8,128)(2,1)} %param.13, f32[1024]{0:T(1024)} %param.17, f32[128]{0:T(128)S(1)} %add_rsqrt_fusion.1), kind=kOutput, calls=%fused_computation.28 | convolution fusion | flops 806223872 | bytes 7344640 | tf_op jit(solution)/shard_map/tr,ird->itd/dot_general | solution.py:66
  93.0 0.7 fusion.50
  93.7 0.7 fusion.49
  94.3 0.7 fusion.48
  95.0 0.7 fusion.47
  95.7 0.7 fusion.46
  96.3 0.7 fusion.45
  97.0 0.7 fusion.44
  97.6 0.7 fusion.43
  98.3 6.7 %all-to-all-start = ((bf16[8,3,128,128]{3,2,1,0:T(8,128)(2,1)}), bf16[8,3,128,128]{3,2,1,0:T(8,128)(2,1)}, u32[]{:S(2)}, u32[]{:S(2)}) async-start(bf16[8,3,128,128]{3,2,1,0:T(8,128)(2,1)} %fusion.43), calls=%async_computation | async-start | bytes 1572864 | tf_op jit(solution)/shard_map/all_to_all | solution.py:73
  105.1 33.8 %all_gather.18 = bf16[1024,32]{0,1:T(8,128)(2,1)} all-gather(bf16[128,32]{0,1:T(8,128)(2,1)S(1)} %copy-done.3), channel_id=1, replica_groups=mesh['ctx'=8,'expert'=32] {'ctx'}, dimensions={0}, use_global_device_ids=true | all-gather | bytes 73728 | tf_op jit(solution)/shard_map/all_gather | solution.py:64
  139.1 0.1 eq.54
  139.2 0.1 reshape_squeeze.15
  139.3 11.5 %all-gather = s32[1,1024]{1,0:T(1,128)S(1)} all-gather(s32[1,128]{1,0:T(1,128)S(1)} %copy-done.6), channel_id=2, replica_groups=mesh['ctx'=8,'expert'=32] {'ctx'}, dimensions={1}, use_global_device_ids=true | all-gather | bytes 4608 | tf_op jit(solution)/shard_map/all_gather | solution.py:58
  150.9 0.5 broadcast.132
  151.4 0.7 reduce.12
  152.1 1.7 reduce-window.6
  153.8 0.3 slice_reduce_fusion
  154.1 0.6 dynamic_slice.11
  154.7 1.9 fusion.55
  156.6 7.5 %while.10 = (s32[]{:T(128)}, bf16[2,512,1,128]{3,1,2,0:T(8,128)(2,1)}, bf16[2,512,1,128]{3,1,2,0:T(8,128)(2,1)}, bf16[1024,1,128]{2,0,1:T(8,128)(2,1)S(1)}, s32[...) while((s32[]{:T(128)}, ...), condition=%wide.region_4.5_spmd, body=%wide.region_1.4_spmd.sunk | while | flops 273742848 | bytes 7100001 | solution.py:38
  156.6 2.0 fusion.66
  158.6 0.5 fusion.67
  159.1 1.2 fusion.68
  160.3 2.0 fusion.66
  162.3 0.5 fusion.67
  162.9 1.2 fusion.68
  164.1 4.2 %all-to-all-start.1 = ((bf16[8,128,128]{2,1,0:T(8,128)(2,1)}), bf16[8,128,128]{2,1,0:T(8,128)(2,1)S(1)}, u32[]{:S(2)}, u32[]{:S(2)}) async-start(bf16[8,128,128]{2,1,0:T(8,128)(2,1)} %bitcast.27), calls=%async_computation.1 | async-start | bytes 524288 | tf_op jit(solution)/shard_map/all_to_all | solution.py:77
  168.4 0.1 reduce_sum.54
  168.6 1.1 fusion.20
  169.7 7.9 %all-to-all-done.1 = bf16[8,128,128]{2,1,0:T(8,128)(2,1)S(1)} async-done(((bf16[8,128,128]{2,1,0:T(8,128)(2,1)}), bf16[8,128,128]{2,1,0:T(8,128)(2,1)S(1)}, u32[]{:S(2)}, u32[]{:S(2)}) %all-to-all-start.1) | async-done | bytes 262176 | tf_op jit(solution)/shard_map/all_to_all | solution.py:77
  177.6 0.9 copy.41
  178.5 11.2 %all-gather.6.cloned.1.call-done = bf16[1024,1024]{0,1:T(8,128)(2,1)} async-done(((bf16[1024,32]{0,1:T(8,128)(2,1)}), bf16[1024,1024]{0,1:T(8,128)(2,1)}) %all-gather.6.cloned.1.call-update) | async-done | bytes 2097168 | tf_op jit(solution)/shard_map/all_gather | solution.py:80
  189.6 2.6 multiply_reduce_fusion
  192.2 0.8 convolution_convert_fusion.1
  193.0 33.3 %all_to_all.34 = bf16[32,32,1024]{2,1,0:T(8,128)(2,1)S(1)} all-to-all(bf16[32,32,1024]{2,1,0:T(8,128)(2,1)S(1)} %bitcast.202), channel_id=1, replica_groups=mesh['ctx'=8,'expert'=32] {'expert'}, dimensions={0} | all-to-all | bytes 4194304 | tf_op jit(solution)/shard_map/all_to_all | solution.py:104
  226.3 8.8 %convolution_bitcast_fusion = f32[32,1,32,2816]{3,2,0,1:T(8,128)S(1)} fusion(bf16[32,32,1024]{2,1,0:T(8,128)(2,1)S(1)} %all_to_all.34, bf16[1,1024,2816]{2,1,0:T(8,128)(2,1)} %param.22), kind=kOutput, calls=%fused_computation.14 | convolution fusion | flops 5905580032 | bytes 19398656 | tf_op jit(solution)/shard_map/sxcd,xdf->sxcf/dot_general | solution.py:107
  235.1 4.9 %fusion.15 = bf16[32,32,1024]{2,1,0:T(8,128)(2,1)} fusion(bf16[1,1408,1024]{2,1,0:T(8,128)(2,1)S(1)} %copy-done, f32[32,1,32,2816]{3,2,0,1:T(8,128)S(1)} %convolution_bitcast_fusion), kind=kOutput, calls=%fused_computation.23 | convolution fusion | flops 2962489344 | bytes 16515072 | tf_op jit(solution)/shard_map/sxcf,xfd->sxcd/dot_general | solution.py:109
  240.0 4.9 %all-to-all-start.3 = ((bf16[32,32,1024]{2,1,0:T(8,128)(2,1)}), bf16[32,32,1024]{2,1,0:T(8,128)(2,1)}, u32[]{:S(2)}, u32[]{:S(2)}) async-start(bf16[32,32,1024]{2,1,0:T(8,128)(2,1)} %fusion.15), calls=%async_computation.3 | async-start | bytes 4194304 | tf_op jit(solution)/shard_map/all_to_all | solution.py:112
  245.0 0.1 mul.167
  245.2 27.6 %all-to-all-done.3 = bf16[32,32,1024]{2,1,0:T(8,128)(2,1)} async-done(((bf16[32,32,1024]{2,1,0:T(8,128)(2,1)}), bf16[32,32,1024]{2,1,0:T(8,128)(2,1)}, u32[]{:S(2)}, u32[]{:S(2)}) %all-to-all-start.3) | async-done | bytes 2097184 | tf_op jit(solution)/shard_map/all_to_all | solution.py:112
  272.8 6.4 %gather_fusion = bf16[768,1024]{1,0:T(8,128)(2,1)} fusion(bf16[1024,1024]{1,0:T(8,128)(2,1)} %bitcast.44, s32[1024]{0:T(1024)S(1)} %pad_clamp_fusion), kind=kCustom, calls=%fused_computation | custom fusion | bytes 3148800 | tf_op jit(solution)/shard_map/jit(_take)/gather | solution.py:115
  279.2 3.7 %gather.7 = bf16[128,6,1024]{2,1,0:T(8,128)(2,1)} reshape(bf16[768,1024]{1,0:T(8,128)(2,1)} %gather_fusion) | data formatting | bytes 3145728 | tf_op jit(solution)/shard_map/jit(_take)/gather | solution.py:115
  282.9 3.4 %copy_select_fusion = bf16[128,6,1024]{2,0,1:T(8,128)(2,1)S(1)} fusion(bf16[128,6,1024]{2,1,0:T(8,128)(2,1)} %gather.7, pred[128,6]{0,1:T(8,128)(4,1)S(1)} %get-tuple-element.104), kind=kLoop, calls=%fused_computation.26 | loop fusion | flops 786432 | bytes 3146496 | tf_op jit(solution)/shard_map/jit(_take)/select_n | solution.py:115
  286.4 1.1 fusion.39
  (39 shorter events, 0.6 us)
Async XLA Ops:
  6.5 228.6 %copy-start = (bf16[1,1408,1024]{2,1,0:T(8,128)(2,1)S(1)}, bf16[1,1408,1024]{2,1,0:T(8,128)(2,1)}, u32[]{:S(2)}) copy-start(bf16[1,1408,1024]{2,1,0:T(8,128)(2,1)} %param.23) | copy-start | bytes 8650756
  6.5 82.5 %all-gather.4.cloned.1.call-start = ((), (), s32[]{:S(2)}) async-start(), calls=%async_computation.4 | async-start | bytes 6488064 | tf_op jit(solution)/shard_map/all_gather | solution.py:69
  93.0 12.1 %copy-start.3 = (bf16[128,32]{0,1:T(8,128)(2,1)S(1)}, bf16[128,32]{0,1:T(8,128)(2,1)}, u32[]{:S(2)}) copy-start(bf16[128,32]{0,1:T(8,128)(2,1)} %param.21) | copy-start | bytes 24580
  93.0 45.9 %copy-start.2 = (s32[1,128,6]{1,0,2:T(1,128)S(1)}, s32[1,128,6]{1,0,2:T(1,128)}, u32[]{:S(2)}) copy-start(s32[1,128,6]{1,0,2:T(1,128)} %param.15) | copy-start | bytes 9220
  93.0 46.3 %copy-start.6 = (s32[1,128]{1,0:T(1,128)S(1)}, s32[1,128]{1,0:T(1,128)}, u32[]{:S(2)}) copy-start(s32[1,128]{1,0:T(1,128)} %param.14) | copy-start | bytes 1540
  93.0 61.1 %copy-start.7 = (f32[8]{0:T(128)S(1)}, f32[8]{0:T(128)}, u32[]{:S(2)}) copy-start(f32[8]{0:T(128)} %param.19) | copy-start | bytes 100
  98.3 56.4 %all-to-all-start = ((bf16[8,3,128,128]{3,2,1,0:T(8,128)(2,1)}), bf16[8,3,128,128]{3,2,1,0:T(8,128)(2,1)}, u32[]{:S(2)}, u32[]{:S(2)}) async-start(bf16[8,3,128,128]{3,2,1,0:T(8,128)(2,1)} %fusion.43), calls=%async_computation | async-start | bytes 1572864 | tf_op jit(solution)/shard_map/all_to_all | solution.py:73
  105.0 84.6 %all-gather.6.cloned.1.call-start = ((), (), s32[]{:S(2)}) async-start(), calls=%async_computation.5 | async-start | bytes 2162688 | tf_op jit(solution)/shard_map/all_gather | solution.py:80
  164.1 13.5 %all-to-all-start.1 = ((bf16[8,128,128]{2,1,0:T(8,128)(2,1)}), bf16[8,128,128]{2,1,0:T(8,128)(2,1)S(1)}, u32[]{:S(2)}, u32[]{:S(2)}) async-start(bf16[8,128,128]{2,1,0:T(8,128)(2,1)} %bitcast.27), calls=%async_computation.1 | async-start | bytes 524288 | tf_op jit(solution)/shard_map/all_to_all | solution.py:77
  168.3 24.0 %copy-start.4 = (f32[1024]{0:T(1024)S(1)}, f32[1024]{0:T(1024)}, u32[]{:S(2)}) copy-start(f32[1024]{0:T(1024)} %param.18) | copy-start | bytes 12292
  189.6 2.6 copy-start.1
  240.0 5.1 %copy-start.5 = (f32[1,128,6]{1,0,2:T(1,128)S(1)}, f32[1,128,6]{1,0,2:T(1,128)}, u32[]{:S(2)}) copy-start(f32[1,128,6]{1,0,2:T(1,128)} %param.16) | copy-start | bytes 9220
  240.0 32.8 %all-to-all-start.3 = ((bf16[32,32,1024]{2,1,0:T(8,128)(2,1)}), bf16[32,32,1024]{2,1,0:T(8,128)(2,1)}, u32[]{:S(2)}, u32[]{:S(2)}) async-start(bf16[32,32,1024]{2,1,0:T(8,128)(2,1)} %fusion.15), calls=%async_computation.3 | async-start | bytes 4194304 | tf_op jit(solution)/shard_map/all_to_all | solution.py:112
Sparse Core Ops, SparseCore 0:
  30.4 58.5 all-gather.3
  139.0 50.5 all-gather.5
